TPU v7x, 32 devices: a whole 2x2x4 slice. The times are simulated.
32 devices in a mesh: band: 4 (over y, x), lon: 8 (over z, core).
Axes of the slice: x: 2, y: 2, z: 4, core: 2. Of those that a mesh axis runs over, the one named last changes fastest.
Arguments:
- sky_maps: float32 [16, 512, 256], P(None, ('band', 'lon')), may hold values from -9 to 9
- noise_var: float32 [512, 256], P(('band', 'lon')), may hold values from 1 to 4
- position: float32 [3, 512, 256], P(None, ('band', 'lon')), may hold values from -1 to 1
- leaf_basis: float32 [512, 256, 64], P(('band', 'lon')), may hold values from -1 to 1
- leaf_couple: float32 [512, 4, 64, 64], P(('band', 'lon')), as said below
- transfer: float32 [512, 64, 64], P(('band', 'lon')), may hold values from -2 to 2
- panel_couple: float32 [64, 2, 64, 64], P(('band', 'lon')), as said below
- near_list: int32 [512, 5], P(('band', 'lon')), may hold values from -1 to 511, as said below
- far_list: int32 [512, 4], P(('band', 'lon')), may hold values from 0 to 511, as said below
- panel_list: int32 [64, 2], P(('band', 'lon')), may hold values from 0 to 63, as said below
- leaf_panel: int32 [512], P(('band', 'lon')), may hold values from 0 to 1
Outputs:
- solution: float32 [16, 512, 256], P(None, ('band', 'lon'))
- residual: float32 [16, 512, 256], P(None, ('band', 'lon'))
Inputs may be any that keep to these rules, and one draw needn't show every extreme that they name: `near_list`: entry 0 of a row is the leaf itself; the entries after it that are not -1 come first and are distinct leaves of the same band at cycle distance 1 or 2, the cycle closing; leaf j stands in leaf i's row exactly when i stands in j's. `far_list`: distinct leaves of the same band at cycle distance 3 to 6, the cycle closing; leaf j stands in leaf i's row exactly when i stands in j's. If leaf j stands in slot s of far_list[i] and leaf i in slot t of far_list[j], then leaf_couple[j, t] is the transpose of leaf_couple[i, s]. `panel_list`: entries are panel s of sectors of other bands at the same longitude (sector ids differing by a nonzero multiple of the sectors of a band), s being the panel's own index in its sector; panel j stands in panel k's row as often as k stands in j's. If panel j stands in slot s of panel_list[k] and these slots pair up with the slots t of panel_list[j] that hold k, then panel_couple[j, t] is the transpose of panel_couple[k, s].
All inputs are finite; a program needn't handle non-finite values.
Results may differ from a plain program's by a relative error of at most 0.0003.
Values sent between devices are 32-bit elements; how exact they have to be, the bound alone decides.
A program may use at most 128 MiB of HBM per device.

v0:
```python
import math

import jax
import jax.numpy as jnp
from jax import lax
from jax.sharding import PartitionSpec as P

REACH = 6
ITERS = 2


HIGHEST_PRECISION = lax.Precision.HIGHEST
ROOT_THREE = math.sqrt(3.0)
AMPLITUDE = 0.02


def extended(cells, sides, width):
    for axis, dim in sides:
        count = lax.axis_size(axis)
        head = lax.slice_in_dim(cells, 0, width, axis=dim)
        tail = lax.slice_in_dim(cells, cells.shape[dim] - width, cells.shape[dim], axis=dim)
        cells = jnp.concatenate(
            [
                lax.ppermute(tail, axis, [(i, (i + 1) % count) for i in range(count)]),
                cells,
                lax.ppermute(head, axis, [((i + 1) % count, i) for i in range(count)]),
            ],
            axis=dim,
        )
    return cells


def matern_block(rows_pos, cols_pos, length_scale):
    squared = jnp.zeros((cols_pos.shape[1], rows_pos.shape[1], cols_pos.shape[2]), jnp.float32)
    for component in range(3):
        offset = rows_pos[component][None, :, None] - cols_pos[component][:, None, :]
        squared = squared + offset * offset
    scaled = ROOT_THREE * jnp.sqrt(squared) / length_scale
    return AMPLITUDE * (1.0 + scaled) * jnp.exp(-scaled)


def on_device(
    sky_maps,
    noise_var,
    position,
    leaf_basis,
    leaf_couple,
    transfer,
    panel_couple,
    near_list,
    far_list,
    panel_list,
    leaf_panel,
):
    lon_index = lax.axis_index("lon")
    lon_count = lax.axis_size("lon")
    local_leaves = sky_maps.shape[1]
    pixel_count = sky_maps.shape[2]
    cycle_size = local_leaves * lon_count
    panel_count = panel_couple.shape[0]
    length_scale = 2.0 * math.pi / cycle_size
    first_leaf = lon_index * local_leaves
    near_depth = 2

    def rim_index(leaf_ids, depth):
        return (leaf_ids % cycle_size - first_leaf + depth) % cycle_size

    near_valid = near_list >= 0
    near_rows = rim_index(jnp.where(near_valid, near_list, near_list[:, :1]), near_depth)
    far_rows = rim_index(far_list, REACH)
    rim_pos = extended(position, (("lon", 1),), near_depth)

    def leaf_blocks(inputs):
        rows_pos, rows_index, slot_mask = inputs
        cols_pos = rim_pos[:, rows_index]
        return matern_block(rows_pos, cols_pos, length_scale) * slot_mask[:, None, None]

    near_blocks = lax.map(
        leaf_blocks, (jnp.transpose(position, (1, 0, 2)), near_rows, near_valid.astype(jnp.float32))
    )
    band_slot = panel_list // (lon_count * panel_count)
    gathered_rows = band_slot * panel_count + panel_list % panel_count
    membership = (leaf_panel[:, None] == jnp.arange(panel_count, dtype=jnp.int32)[None, :]).astype(
        jnp.float32
    )

    def square_total(vector):
        return lax.psum(jnp.sum(vector * vector, axis=(1, 2)), ("band", "lon"))

    solution = jnp.zeros_like(sky_maps)
    residual = sky_maps
    direction = sky_maps
    norm_now = square_total(residual)
    for iteration in range(ITERS):
        coeffs = jnp.einsum("lpr,mlp->mlr", leaf_basis, direction, precision=HIGHEST_PRECISION)
        joined = jnp.concatenate([direction, coeffs], axis=2)
        rim_joined = extended(joined, (("lon", 1),), REACH)
        rim_values = rim_joined[
            :, REACH - near_depth : REACH + local_leaves + near_depth, :pixel_count
        ]
        rim_coeffs = rim_joined[:, :, pixel_count:]
        near_part = jnp.einsum(
            "lspq,mlsq->mlp", near_blocks, rim_values[:, near_rows], precision=HIGHEST_PRECISION
        )
        leaf_far = jnp.einsum(
            "lsab,mlsb->mla", leaf_couple, rim_coeffs[:, far_rows], precision=HIGHEST_PRECISION
        )
        upward = jnp.einsum("lab,mla->mlb", transfer, coeffs, precision=HIGHEST_PRECISION)
        panel_coeffs = jnp.einsum("lk,mlb->mkb", membership, upward, precision=HIGHEST_PRECISION)
        band_coeffs = lax.all_gather(panel_coeffs, "band", axis=1, tiled=True)
        panel_far = jnp.einsum(
            "ksab,mksb->mka",
            panel_couple,
            band_coeffs[:, gathered_rows],
            precision=HIGHEST_PRECISION,
        )
        downward = jnp.einsum("lk,mkb->mlb", membership, panel_far, precision=HIGHEST_PRECISION)
        leaf_far = leaf_far + jnp.einsum(
            "lab,mlb->mla", transfer, downward, precision=HIGHEST_PRECISION
        )
        far_part = jnp.einsum("lpr,mlr->mlp", leaf_basis, leaf_far, precision=HIGHEST_PRECISION)
        applied = noise_var[None] * direction + near_part + far_part
        curvature_sum = lax.psum(jnp.sum(direction * applied, axis=(1, 2)), ("band", "lon"))
        step_size = norm_now / curvature_sum
        solution = solution + step_size[:, None, None] * direction
        residual = residual - step_size[:, None, None] * applied
        if iteration + 1 < ITERS:
            norm_next = square_total(residual)
            direction = residual + (norm_next / norm_now)[:, None, None] * direction
            norm_now = norm_next
    return (solution, residual)


def solution(mesh):
    placed = (
        P(None, ("band", "lon"), None),
        P(("band", "lon"), None),
        P(None, ("band", "lon"), None),
        P(("band", "lon"), None, None),
        P(("band", "lon"), None, None, None),
        P(("band", "lon"), None, None),
        P(("band", "lon"), None, None, None),
        P(("band", "lon"), None),
        P(("band", "lon"), None),
        P(("band", "lon"), None),
        P(("band", "lon")),
    )
    return jax.shard_map(
        on_device,
        mesh=mesh,
        in_specs=placed,
        out_specs=(P(None, ("band", "lon"), None), P(None, ("band", "lon"), None)),
        check_vma=False,
    )
```

profile of v0, /device:TPU:0, one launch (start us, length us, event | category | flops | bytes accessed | tf_op | source)
XLA Modules:
  0.0 338.2 jit_solution(1324959199199054812)
XLA Ops:
  2.7 4.1 %collective-permute-start.3 = (f32[3,2,256]{2,0,1:T(4,128)S(1)}, f32[3,2,256]{2,0,1:T(4,128)}, u32[]{:S(2)}, u32[]{:S(2)}) collective-permute-start(f32[3,2,256]{2,0,1:T(4,128)S(1)} %get-tuple-element.117), channel_id=1, source_target_pairs={{1,0},{2,1},{3,2},{4,3},{5,4},{6,5},{7,6},{0,7},{9,8},{10,9},{11,1... | collective-permute-start | bytes 18440 | tf_op jit(solution)/shard_map/ppermute | solution.py:26
  8.0 2.4 convolution_bitcast_fusion.11
  11.1 3.5 %collective-permute-start.1 = (f32[16,6,320]{2,0,1:T(8,128)}, f32[16,6,320]{2,0,1:T(8,128)}, u32[]{:S(2)}, u32[]{:S(2)}) collective-permute-start(f32[16,6,320]{2,0,1:T(8,128)} %get-tuple-element.113), channel_id=1, source_target_pairs={{1,0},{2,1},{3,2},{4,3},{5,4},{6,5},{7,6},{0,7},{9,8},{10,9},{11,1... | collective-permute-start | bytes 368648 | tf_op jit(solution)/shard_map/ppermute | solution.py:26
  18.5 8.7 %all_gather.6 = f32[16,8,64]{2,0,1:T(8,128)S(1)} all-gather(f32[16,2,64]{2,0,1:T(8,128)S(1)} %copy.56), channel_id=1, replica_groups=mesh['band'=4,'lon'=8] {'band'}, dimensions={1}, use_global_device_ids=true | all-gather | bytes 40960 | tf_op jit(solution)/shard_map/all_gather | solution.py:110
  33.1 97.9 %while.12 = (s32[]{:T(128)}, f32[16,5,256,256]{3,2,1,0:T(8,128)}, f32[16,3,256]{2,1,0:T(4,128)}, s32[16,5]{1,0:T(8,128)S(1)}, f32[3,20,256]{2,0,1:T(4,128)S(1)},...) while((s32[]{:T(128)}, f32[16,5,256,256]{3,2,1,0:T(8,128)}, f32[16,3,256]{2,1,0:T(4,128)}, ...), condition=%wide.region_3.4_spmd, body=%wide.region_2.3_spmd.sunk | while | flops 4588563 | bytes 1434957 | solution.py:78
  34.6 1.4 constant_dynamic-slice_fusion.6
  36.6 2.8 multiply_dynamic-update-slice_fusion.2
  39.4 1.2 fusion.64
  40.7 1.4 constant_dynamic-slice_fusion.6
  42.7 2.8 multiply_dynamic-update-slice_fusion.2
  45.5 1.2 fusion.64
  46.8 1.4 constant_dynamic-slice_fusion.6
  48.8 2.8 multiply_dynamic-update-slice_fusion.2
  52.9 1.4 constant_dynamic-slice_fusion.6
  54.9 2.8 multiply_dynamic-update-slice_fusion.2
  59.0 1.4 constant_dynamic-slice_fusion.6
  61.0 2.8 multiply_dynamic-update-slice_fusion.2
  65.1 1.4 constant_dynamic-slice_fusion.6
  67.1 2.8 multiply_dynamic-update-slice_fusion.2
  71.2 1.4 constant_dynamic-slice_fusion.6
  73.2 2.9 multiply_dynamic-update-slice_fusion.2
  77.3 1.4 constant_dynamic-slice_fusion.6
  79.4 2.8 multiply_dynamic-update-slice_fusion.2
  82.2 1.2 fusion.64
  83.5 1.4 constant_dynamic-slice_fusion.6
  85.5 2.8 multiply_dynamic-update-slice_fusion.2
  88.3 1.2 fusion.64
  89.5 1.4 constant_dynamic-slice_fusion.6
  91.6 2.9 multiply_dynamic-update-slice_fusion.2
  94.4 1.2 fusion.64
  95.7 1.4 constant_dynamic-slice_fusion.6
  97.7 2.8 multiply_dynamic-update-slice_fusion.2
  100.5 1.2 fusion.64
  101.8 1.4 constant_dynamic-slice_fusion.6
  103.8 2.8 multiply_dynamic-update-slice_fusion.2
  106.6 1.2 fusion.64
  107.9 1.4 constant_dynamic-slice_fusion.6
  109.9 2.8 multiply_dynamic-update-slice_fusion.2
  112.7 1.2 fusion.64
  114.0 1.4 constant_dynamic-slice_fusion.6
  116.0 2.9 multiply_dynamic-update-slice_fusion.2
  118.8 1.2 fusion.64
  120.1 1.4 constant_dynamic-slice_fusion.6
  122.1 2.8 multiply_dynamic-update-slice_fusion.2
  124.9 1.2 fusion.64
  126.2 1.4 constant_dynamic-slice_fusion.6
  128.2 2.8 multiply_dynamic-update-slice_fusion.2
  131.0 1.6 pad_maximum_fusion.5
  132.6 2.5 gather_fusion.2
  135.1 2.9 convolution_bitcast_fusion.9
  138.0 1.6 fusion.8
  140.4 1.8 gather_fusion.1
  142.2 21.5 %fusion.6 = f32[16,16,256]{2,0,1:T(8,128)S(1)} fusion(f32[16,16,5,256]{3,0,2,1:T(8,128)} %bitcast.154, f32[16,5,256,256]{3,2,1,0:T(8,128)} %get-tuple-element.79, f32[16,256]{1,0:T(8,128)S(1)} %copy-done.23, f32[16,16,256]{2,1,0:T(8,128)S(1)} %copy-done.1), kind=kOutput, calls=%fused_computation.28 | convolution fusion | flops 1006764032 | bytes 22822912 | tf_op jit(solution)/shard_map/lspq,mlsq->mlp/dot_general | solution.py:102
  164.5 37.1 %all-reduce = (f32[16]{0:T(128)S(1)}, f32[16]{0:T(128)S(1)}) all-reduce(f32[16]{0:T(128)S(1)} %copy-done.33, f32[16]{0:T(128)S(1)} %get-tuple-element.120), channel_id=1, replica_groups=mesh['band'=4,'lon'=8] {'band','lon'}, use_global_device_ids=true, to_apply=%region_1.2 | all-reduce | flops 32 | bytes 256 | tf_op jit(solution)/shard_map/psum | solution.py:88
  201.9 42.3 %psum.30 = f32[16]{0:T(128)S(1)} all-reduce(f32[16]{0:T(128)S(1)} %multiply_reduce_fusion.1), channel_id=1, replica_groups=mesh['band'=4,'lon'=8] {'band','lon'}, use_global_device_ids=true, to_apply=%region_7.8 | all-reduce | flops 16 | bytes 128 | tf_op jit(solution)/shard_map/psum | solution.py:88
  244.5 2.2 convolution_bitcast_fusion.10
  248.2 9.0 %all_gather.7 = f32[16,8,64]{2,0,1:T(8,128)S(1)} all-gather(f32[16,2,64]{2,0,1:T(8,128)S(1)} %copy.64), channel_id=1, replica_groups=mesh['band'=4,'lon'=8] {'band'}, dimensions={1}, use_global_device_ids=true | all-gather | bytes 40960 | tf_op jit(solution)/shard_map/all_gather | solution.py:110
  259.1 3.5 %collective-permute-start.5 = (f32[16,6,320]{2,0,1:T(8,128)S(1)}, f32[16,6,320]{2,0,1:T(8,128)S(1)}, u32[]{:S(2)}, u32[]{:S(2)}) collective-permute-start(f32[16,6,320]{2,0,1:T(8,128)S(1)} %get-tuple-element.111), channel_id=1, source_target_pairs={{1,0},{2,1},{3,2},{4,3},{5,4},{6,5},{7,6},{0,7},{9,8},{10,9},{11,1... | collective-permute-start | bytes 368648 | tf_op jit(solution)/shard_map/ppermute | solution.py:26
  263.5 3.5 %collective-permute-done.4 = f32[16,6,320]{2,0,1:T(8,128)S(1)} collective-permute-done((f32[16,6,320]{2,0,1:T(8,128)}, f32[16,6,320]{2,0,1:T(8,128)S(1)}, u32[]{:S(2)}, u32[]{:S(2)}) %collective-permute-start.4) | collective-permute-done | bytes 122912 | tf_op jit(solution)/shard_map/ppermute | solution.py:24
  269.3 1.5 gather_fusion.5
  270.8 3.6 %convolution_bitcast_fusion.6 = f32[16,16,64]{2,1,0:T(8,128)} fusion(f32[16,16,4,64]{3,0,2,1:T(8,128)} %bitcast.155, f32[16,4,64,64]{3,2,1,0:T(8,128)S(1)} %copy-done), kind=kOutput, calls=%fused_computation.33 | convolution fusion | flops 50331648 | bytes 1376256 | tf_op jit(solution)/shard_map/lsab,mlsb->mla/dot_general | solution.py:105
  274.4 1.8 gather_fusion.4
  276.2 21.5 %fusion.5 = f32[16,16,256]{2,0,1:T(8,128)S(1)} fusion(f32[16,16,5,256]{3,0,2,1:T(8,128)} %bitcast.153, f32[16,5,256,256]{3,2,1,0:T(8,128)} %get-tuple-element.79, f32[16,16,256]{2,0,1:T(8,128)S(1)} %multiply_add_fusion.1, f32[16,256]{1,0:T(8,128)S(1)} %copy-done.23), kind=kOutput, calls=%fused_computation.26 | convolution fusion | flops 1006764032 | bytes 22822912 | tf_op jit(solution)/shard_map/lspq,mlsq->mlp/dot_general | solution.py:102
  299.4 36.9 %psum.31 = f32[16]{0:T(128)S(1)} all-reduce(f32[16]{0:T(128)S(1)} %get-tuple-element.122), channel_id=1, replica_groups=mesh['band'=4,'lon'=8] {'band','lon'}, use_global_device_ids=true, to_apply=%region_9.10 | all-reduce | flops 16 | bytes 128 | tf_op jit(solution)/shard_map/psum | solution.py:123
  (285 shorter events, 43.3 us)
Async XLA Ops:
  0.6 134.4 %copy-start = (f32[16,4,64,64]{3,2,1,0:T(8,128)S(1)}, f32[16,4,64,64]{3,2,1,0:T(8,128)}, u32[]{:S(2)}) copy-start(f32[16,4,64,64]{3,2,1,0:T(8,128)} %param.17) | copy-start | bytes 3145732
  2.3 29.4 %collective-permute-start.2 = (f32[3,2,256]{2,0,1:T(4,128)}, f32[3,2,256]{2,0,1:T(4,128)S(1)}, u32[]{:S(2)}, u32[]{:S(2)}) collective-permute-start(f32[3,2,256]{2,0,1:T(4,128)} %get-tuple-element.116), channel_id=1, source_target_pairs={{0,1},{1,2},{2,3},{3,4},{4,5},{5,6},{6,7},{7,0},{8,9},{9,10},{10,1... | collective-permute-start | bytes 18440 | tf_op jit(solution)/shard_map/ppermute | solution.py:24
  2.7 12.0 %copy-start.1 = (f32[16,16,256]{2,1,0:T(8,128)S(1)}, f32[16,16,256]{2,1,0:T(8,128)}, u32[]{:S(2)}) copy-start(f32[16,16,256]{2,1,0:T(8,128)} %param.13) | copy-start | bytes 786436
  2.7 29.5 %collective-permute-start.3 = (f32[3,2,256]{2,0,1:T(4,128)S(1)}, f32[3,2,256]{2,0,1:T(4,128)}, u32[]{:S(2)}, u32[]{:S(2)}) collective-permute-start(f32[3,2,256]{2,0,1:T(4,128)S(1)} %get-tuple-element.117), channel_id=1, source_target_pairs={{1,0},{2,1},{3,2},{4,3},{5,4},{6,5},{7,6},{0,7},{9,8},{10,9},{11,1... | collective-permute-start | bytes 18440 | tf_op jit(solution)/shard_map/ppermute | solution.py:26
  7.9 7.6 %copy-start.30 = (s32[16,5]{0,1:T(8,128)S(1)}, s32[16,5]{0,1:T(8,128)}, u32[]{:S(2)}) copy-start(s32[16,5]{0,1:T(8,128)} %param.20) | copy-start | bytes 964
  7.9 7.7 %copy-start.32 = (s32[2,2]{1,0:T(2,128)S(1)}, s32[2,2]{1,0:T(2,128)}, u32[]{:S(2)}) copy-start(s32[2,2]{1,0:T(2,128)} %param.22) | copy-start | bytes 52
  7.9 7.8 %copy-start.31 = (s32[16,4]{0,1:T(4,128)S(1)}, s32[16,4]{0,1:T(4,128)}, u32[]{:S(2)}) copy-start(s32[16,4]{0,1:T(4,128)} %param.21) | copy-start | bytes 772
  7.9 9.8 %copy-start.4 = (f32[16,64,64]{2,1,0:T(8,128)S(1)}, f32[16,64,64]{2,1,0:T(8,128)}, u32[]{:S(2)}) copy-start(f32[16,64,64]{2,1,0:T(8,128)} %param.18) | copy-start | bytes 786436
  8.0 10.4 %copy-start.25 = (s32[16]{0:T(128)S(1)}, s32[16]{0:T(128)}, u32[]{:S(2)}) copy-start(s32[16]{0:T(128)} %param.23) | copy-start | bytes 196
  10.4 120.7 %copy-start.7 = (f32[16,16,64]{2,0,1:T(8,128)}, f32[16,16,64]{2,0,1:T(8,128)S(1)}, u32[]{:S(2)}) copy-start(f32[16,16,64]{2,0,1:T(8,128)S(1)} %convolution_bitcast_fusion.11) | copy-start | bytes 196612
  11.1 119.9 %collective-permute-start = (f32[16,6,320]{2,0,1:T(8,128)}, f32[16,6,320]{2,0,1:T(8,128)S(1)}, u32[]{:S(2)}, u32[]{:S(2)}) collective-permute-start(f32[16,6,320]{2,0,1:T(8,128)} %get-tuple-element.112), channel_id=1, source_target_pairs={{0,1},{1,2},{2,3},{3,4},{4,5},{5,6},{6,7},{7,0},{8,9},{9,10},{10,1... | collective-permute-start | bytes 368648 | tf_op jit(solution)/shard_map/ppermute | solution.py:24
  11.1 119.9 %collective-permute-start.1 = (f32[16,6,320]{2,0,1:T(8,128)}, f32[16,6,320]{2,0,1:T(8,128)}, u32[]{:S(2)}, u32[]{:S(2)}) collective-permute-start(f32[16,6,320]{2,0,1:T(8,128)} %get-tuple-element.113), channel_id=1, source_target_pairs={{1,0},{2,1},{3,2},{4,3},{5,4},{6,5},{7,6},{0,7},{9,8},{10,9},{11,1... | collective-permute-start | bytes 368648 | tf_op jit(solution)/shard_map/ppermute | solution.py:26
  15.7 17.5 %copy-start.24 = (s32[1024]{0:T(1024)}, s32[1024]{0:T(1024)S(1)}, u32[]{:S(2)}) copy-start(s32[1024]{0:T(1024)S(1)} %pad_clamp_fusion.1) | copy-start | bytes 12292
  33.3 3.2 copy-start.27
  36.6 2.8 copy-start.28
  39.4 3.2 copy-start.27
  42.7 2.8 copy-start.28
  45.5 3.2 copy-start.27
  48.8 2.8 copy-start.28
  51.6 3.2 copy-start.27
  54.9 2.9 copy-start.28
  57.8 3.2 copy-start.27
  61.0 2.8 copy-start.28
  63.8 3.2 copy-start.27
  67.1 2.8 copy-start.28
  69.9 3.2 copy-start.27
  73.2 2.9 copy-start.28
  76.1 3.2 copy-start.27
  79.3 2.9 copy-start.28
  82.2 3.2 copy-start.27
  85.5 2.8 copy-start.28
  88.3 3.2 copy-start.27
  91.5 2.9 copy-start.28
  94.4 3.2 copy-start.27
  97.7 2.8 copy-start.28
  100.5 3.2 copy-start.27
  103.8 2.9 copy-start.28
  106.6 3.2 copy-start.27
  109.9 2.8 copy-start.28
  112.7 3.2 copy-start.27
  116.0 2.9 copy-start.28
  118.8 3.2 copy-start.27
  122.1 2.8 copy-start.28
  124.9 3.2 copy-start.27
  128.2 2.8 copy-start.28
  131.0 6.9 %copy-start.11 = (f32[16,6,320]{2,0,1:T(8,128)}, f32[16,6,320]{2,0,1:T(8,128)S(1)}, u32[]{:S(2)}) copy-start(f32[16,6,320]{2,0,1:T(8,128)S(1)} %collective-permute-done) | copy-start | bytes 368644
  135.1 2.9 copy-start.17
  135.1 4.5 %copy-start.8 = (f32[16,16,64]{2,0,1:T(8,128)S(1)}, f32[16,16,64]{2,0,1:T(8,128)}, u32[]{:S(2)}) copy-start(f32[16,16,64]{2,0,1:T(8,128)} %copy-done.7) | copy-start | bytes 196612
  138.0 2.4 copy-start.22
  140.4 1.8 copy-start.23
  142.2 21.5 %copy-start.2 = (f32[16,256,64]{1,2,0:T(8,128)S(1)}, f32[16,256,64]{1,2,0:T(8,128)}, u32[]{:S(2)}) copy-start(f32[16,256,64]{1,2,0:T(8,128)} %param.16) | copy-start | bytes 3145732
  142.2 21.5 %copy-start.16 = (f32[16,16,64]{2,0,1:T(8,128)S(1)}, f32[16,16,64]{2,0,1:T(8,128)}, u32[]{:S(2)}) copy-start(f32[16,16,64]{2,0,1:T(8,128)} %fusion.8) | copy-start | bytes 196612
  164.5 82.1 %copy-start.5 = (f32[16,16,256]{2,0,1:T(8,128)}, f32[16,16,256]{2,0,1:T(8,128)S(1)}, u32[]{:S(2)}) copy-start(f32[16,16,256]{2,0,1:T(8,128)S(1)} %get-tuple-element.121) | copy-start | bytes 786436
  244.5 3.6 %copy-start.26 = (s32[16]{0:T(128)S(1)}, s32[16]{0:T(128)}, u32[]{:S(2)}) copy-start(s32[16]{0:T(128)} %param.23) | copy-start | bytes 196
  247.3 22.0 %copy-start.21 = (s32[1024]{0:T(1024)S(1)}, s32[1024]{0:T(1024)}, u32[]{:S(2)}) copy-start(s32[1024]{0:T(1024)} %pad_clamp_fusion.2) | copy-start | bytes 12292
  259.0 8.0 %collective-permute-start.4 = (f32[16,6,320]{2,0,1:T(8,128)}, f32[16,6,320]{2,0,1:T(8,128)S(1)}, u32[]{:S(2)}, u32[]{:S(2)}) collective-permute-start(f32[16,6,320]{2,0,1:T(8,128)} %get-tuple-element.110), channel_id=1, source_target_pairs={{0,1},{1,2},{2,3},{3,4},{4,5},{5,6},{6,7},{7,0},{8,9},{9,10},{10,1... | collective-permute-start | bytes 368648 | tf_op jit(solution)/shard_map/ppermute | solution.py:24
  259.1 8.0 %collective-permute-start.5 = (f32[16,6,320]{2,0,1:T(8,128)S(1)}, f32[16,6,320]{2,0,1:T(8,128)S(1)}, u32[]{:S(2)}, u32[]{:S(2)}) collective-permute-start(f32[16,6,320]{2,0,1:T(8,128)S(1)} %get-tuple-element.111), channel_id=1, source_target_pairs={{1,0},{2,1},{3,2},{4,3},{5,4},{6,5},{7,6},{0,7},{9,8},{10,9},{11,1... | collective-permute-start | bytes 368648 | tf_op jit(solution)/shard_map/ppermute | solution.py:26
  270.8 3.6 %copy-start.10 = (f32[16,16,64]{2,0,1:T(8,128)S(1)}, f32[16,16,64]{2,0,1:T(8,128)}, u32[]{:S(2)}) copy-start(f32[16,16,64]{2,0,1:T(8,128)} %copy-done.9) | copy-start | bytes 196612
  270.8 3.6 %copy-start.13 = (f32[16,6,320]{2,0,1:T(8,128)S(1)}, f32[16,6,320]{2,0,1:T(8,128)}, u32[]{:S(2)}) copy-start(f32[16,6,320]{2,0,1:T(8,128)} %copy-done.12) | copy-start | bytes 368644
  270.8 3.6 %copy-start.15 = (f32[16,6,320]{2,0,1:T(8,128)S(1)}, f32[16,6,320]{2,0,1:T(8,128)}, u32[]{:S(2)}) copy-start(f32[16,6,320]{2,0,1:T(8,128)} %copy-done.14) | copy-start | bytes 368644
  276.2 21.5 %copy-start.18 = (f32[16,16,64]{2,1,0:T(8,128)S(1)}, f32[16,16,64]{2,1,0:T(8,128)}, u32[]{:S(2)}) copy-start(f32[16,16,64]{2,1,0:T(8,128)} %convolution_bitcast_fusion.4) | copy-start | bytes 196612
  276.2 21.5 %copy-start.19 = (f32[16,16,64]{2,1,0:T(8,128)S(1)}, f32[16,16,64]{2,1,0:T(8,128)}, u32[]{:S(2)}) copy-start(f32[16,16,64]{2,1,0:T(8,128)} %convolution_bitcast_fusion.6) | copy-start | bytes 196612
  276.2 22.4 %copy-start.3 = (f32[16,256,64]{1,2,0:T(8,128)S(1)}, f32[16,256,64]{1,2,0:T(8,128)}, u32[]{:S(2)}) copy-start(f32[16,256,64]{1,2,0:T(8,128)} %param.16) | copy-start | bytes 3145732
  297.7 38.6 %copy-start.6 = (f32[16,16,256]{2,0,1:T(8,128)S(1)}, f32[16,16,256]{2,0,1:T(8,128)}, u32[]{:S(2)}) copy-start(f32[16,16,256]{2,0,1:T(8,128)} %copy-done.5) | copy-start | bytes 786436
  (6 other events, 4.5 us)
where the time goes:
time: 342 us; the launch traced here: 338 us
  blocking collectives  134 us (39%)
  local copies, waits for them, and re-layouts  68.4 us (20%)
  matrix products  63.6 us (19%)
  other arithmetic  55 us (16%)
  starting transfers between devices  11.7 us (3%)
  waiting for transfers between devices  3.56 us (1%)
    psum x2, blocking collectives, square_total(): return lax.psum(jnp.sum(vector * vector, axis=(1, 2)), ('band', 'lon'))  79.5 us
    dynamic_update_slice x16, other arithmetic, on_device(): lax.map(leaf_blocks, (jnp.transpose(position, (1, 0, 2)), near_rows, near...  45.2 us
    dot_general x2, matrix products, on_device(): jnp.einsum('lspq,mlsq->mlp', near_blocks, rim_values[:, near_rows], preci...  42.9 us
    psum x1, blocking collectives, on_device(): lax.psum(jnp.sum(direction * applied, axis=(1, 2)), ('band', 'lon'))  36.9 us
    slice x16, local copies, waits for them, and re-layouts, matern_block(): rows_pos[component][None, :, None] - cols_pos[component][:, None, :]  22 us
    mul x16, local copies, waits for them, and re-layouts, leaf_blocks(): matern_block(rows_pos, cols_pos, length_scale) * slot_mask[:, None, None]  20 us
    all_gather x2, blocking collectives, on_device(): band_coeffs = lax.all_gather(panel_coeffs, 'band', axis=1, tiled=True)  17.7 us
    ppermute x3, starting transfers between devices, extended(): lax.ppermute(head, axis, [((i + 1) % count, i) for i in range(count)])  11.2 us
  transfers between devices with their start and end apart: 6, of which 1 were waited for; matrix products, arithmetic and copies ran while one was open for 33% of the time, Pallas kernels for 0%

commit v1 on v0

v1 whole, which is shorter than its diff:
```python
import functools
import math

import jax
import jax.numpy as jnp
from jax import lax
from jax.experimental import pallas as pl
from jax.experimental.pallas import tpu as pltpu
from jax.sharding import PartitionSpec as P

REACH = 6
DEPTH = 2
AMPLITUDE = 0.02
F32 = jnp.float32
BF16 = jnp.bfloat16
NN = (((1,), (0,)), ((), ()))
NT = (((1,), (1,)), ((), ()))
MESH = pl.DeviceIdType.MESH
GROUP = 4


def halves(x):
    hi = x.astype(BF16)
    lo = (x - hi.astype(F32)).astype(BF16)
    return hi, lo


def dot3(a, bhi, blo, dims):
    n = a.shape[0]
    hi, lo = halves(a)
    both = lax.dot_general(
        jnp.concatenate([hi, lo], axis=0), bhi, dims, preferred_element_type=F32
    )
    rest = lax.dot_general(hi, blo, dims, preferred_element_type=F32)
    return both[:n] + both[n:] + rest


def kernel(
    cycle,
    n_lon,
    n_band,
    pos_ref,
    sky_ref,
    noise_ref,
    basis_ref,
    couple_ref,
    transfer_ref,
    pcouple_ref,
    near_ref,
    far_ref,
    plist_ref,
    home_ref,
    sol_ref,
    res_ref,
    posx,
    posc,
    v0,
    v1,
    w2,
    c0,
    c1,
    pc0,
    pc1,
    pf,
    vs,
    khi,
    klo,
    bhi,
    blo,
    whi,
    wlo,
    thi,
    tlo,
    ghi,
    glo,
    red_lon,
    red_band,
    send_sem,
    recv_sem,
):
    leaves, maps, pixels = sky_ref.shape
    rank = basis_ref.shape[2]
    panels = pcouple_ref.shape[0]
    slots = far_ref.shape[1]
    near_slots = near_ref.shape[1]
    lon = lax.axis_index("lon")
    band = lax.axis_index("band")
    right = lax.rem(lon + 1, n_lon)
    left = lax.rem(lon + n_lon - 1, n_lon)
    first = band * cycle + lon * leaves
    used = [0]

    def push(src, dst, target):
        at = used[0]
        used[0] += 1
        copy = pltpu.make_async_remote_copy(
            src_ref=src,
            dst_ref=dst,
            send_sem=send_sem.at[at],
            recv_sem=recv_sem.at[at],
            device_id=target,
            device_id_type=MESH,
        )
        copy.start()
        return copy

    def rim_push(buf, depth):
        return [
            push(buf.at[pl.ds(leaves, depth)], buf.at[pl.ds(0, depth)], {"lon": right}),
            push(
                buf.at[pl.ds(depth, depth)],
                buf.at[pl.ds(depth + leaves, depth)],
                {"lon": left},
            ),
        ]

    def axis_push(buf, axis, me, count):
        return [
            push(buf.at[me], buf.at[me], {axis: lax.rem(me + k, count)}) for k in range(1, count)
        ]

    def landed(copies):
        for copy in copies:
            copy.wait_recv()

    pending = []

    barrier = pltpu.get_barrier_semaphore()
    for k in range(1, n_lon):
        pl.semaphore_signal(
            barrier, inc=1, device_id={"lon": lax.rem(lon + k, n_lon)}, device_id_type=MESH
        )
    for k in range(1, n_band):
        pl.semaphore_signal(
            barrier, inc=1, device_id={"band": lax.rem(band + k, n_band)}, device_id_type=MESH
        )
    posx[pl.ds(DEPTH, leaves)] = pos_ref[...]
    v0[pl.ds(DEPTH, leaves)] = sky_ref[...]
    pl.semaphore_wait(barrier, n_lon - 1 + n_band - 1)
    pos_copies = rim_push(posx, DEPTH)
    v0_copies = rim_push(v0, DEPTH)
    pending += pos_copies + v0_copies

    def prepare(i):
        bhi[i], blo[i] = halves(basis_ref[i])
        thi[i], tlo[i] = halves(transfer_ref[i])
        for s in range(slots):
            whi[i, s], wlo[i, s] = halves(couple_ref[i, s])

    def upward(i, value, cx, sums):
        c = dot3(value, bhi[i], blo[i], NN)
        cx[REACH + i] = c
        up = dot3(c, thi[i], tlo[i], NN)
        home = home_ref[0, i]
        return [sums[k] + up * jnp.where(home == k, 1.0, 0.0).astype(F32) for k in range(panels)]

    zero_panels = [jnp.zeros((maps, rank), F32) for _ in range(panels)]

    def first_coeffs(g, sums):
        for u in range(GROUP):
            prepare(g * GROUP + u)
        for u in range(GROUP):
            i = g * GROUP + u
            sums = upward(i, sky_ref[i], c0, sums)
        return sums

    sums = lax.fori_loop(0, leaves // GROUP, first_coeffs, zero_panels)
    for k in range(panels):
        pc0[band, k] = sums[k]
    c0_copies = rim_push(c0, REACH)
    pc0_copies = axis_push(pc0, "band", band, n_band)
    pending += c0_copies + pc0_copies
    for k in range(panels):
        for s in range(plist_ref.shape[1]):
            ghi[k, s], glo[k, s] = halves(pcouple_ref[k, s])

    landed(pos_copies + v0_copies)
    scale = math.sqrt(3.0) / (2.0 * math.pi / cycle)

    def columns(j, carry):
        scaled = posx[j] * scale
        posx_scaled = scaled
        posc[j] = jnp.transpose(posx_scaled)
        hi, lo = halves(v0[j])
        vs[j, pl.ds(0, maps)] = hi
        vs[j, pl.ds(maps, maps)] = lo
        return carry

    lax.fori_loop(0, leaves + 2 * DEPTH, columns, 0)

    def near_product(i):
        values = jnp.concatenate([vs[i + d] for d in range(2 * DEPTH + 1)], axis=1)
        both = lax.dot_general(values, khi[i], NN, preferred_element_type=F32)
        rest = lax.dot_general(values[:maps], klo[i], NN, preferred_element_type=F32)
        return both[:maps] + both[maps:] + rest

    chunk = 64

    def first_near(i, carry):
        rows = posx[DEPTH + i] * scale
        me = near_ref[i, 0]
        for d in range(2 * DEPTH + 1):
            offset = d - DEPTH
            if offset == 0:
                weight = jnp.asarray(AMPLITUDE, F32)
            else:
                weight = jnp.asarray(0.0, F32)
                for s in range(1, near_slots):
                    other = near_ref[i, s]
                    gap = other - me
                    hit = (gap == offset) | (gap == offset - cycle) | (gap == offset + cycle)
                    weight = weight + jnp.where((other >= 0) & hit, AMPLITUDE, 0.0).astype(F32)
            for q in range(0, pixels, chunk):
                squared = None
                for component in range(3):
                    gap = (
                        posc[i + d, pl.ds(q, chunk), component : component + 1]
                        - rows[component : component + 1]
                    )
                    squared = gap * gap if squared is None else squared + gap * gap
                t = squared * lax.rsqrt(jnp.maximum(squared, 1e-30))
                block = (weight + weight * t) * jnp.exp(-t)
                hi, lo = halves(block)
                khi[i, pl.ds(d * pixels + q, chunk)] = hi
                klo[i, pl.ds(d * pixels + q, chunk)] = lo
        v1[DEPTH + i] = noise_ref[pl.ds(i, 1)] * sky_ref[i] + near_product(i)
        return carry

    lax.fori_loop(0, leaves, first_near, 0)

    def panel_far(pcx):
        for k in range(panels):
            total = jnp.zeros((maps, rank), F32)
            for s in range(plist_ref.shape[1]):
                other = plist_ref[k, s] // (n_lon * panels)
                total = total + dot3(pcx[other, k], ghi[k, s], glo[k, s], NT)
            pf[k] = total

    def far(i, cx):
        total = dot3(pf[home_ref[0, i]], thi[i], tlo[i], NT)
        for s in range(slots):
            gap = far_ref[i, s] - (first + i)
            gap = jnp.where(gap > REACH, gap - cycle, gap)
            gap = jnp.where(gap < -REACH, gap + cycle, gap)
            row = jnp.clip(i + REACH + gap, 0, leaves + 2 * REACH - 1)
            total = total + dot3(cx[row], whi[i, s], wlo[i, s], NT)
        return dot3(total, bhi[i], blo[i], NT)

    landed(c0_copies + pc0_copies)
    panel_far(pc0)
    zero = jnp.zeros((maps, pixels), F32)

    def first_far(g, carry):
        sums, rr, pw, ww = carry
        out = []
        for u in range(GROUP):
            i = g * GROUP + u
            w = v1[DEPTH + i] + far(i, c0)
            v1[DEPTH + i] = w
            p = sky_ref[i]
            rr, pw, ww = rr + p * p, pw + p * w, ww + w * w
            out.append(w)
        for u in range(GROUP):
            sums = upward(g * GROUP + u, out[u], c1, sums)
        return sums, rr, pw, ww

    sums, rr, pw, ww = lax.fori_loop(
        0, leaves // GROUP, first_far, (zero_panels, zero, zero, zero)
    )
    v1_copies = rim_push(v1, DEPTH)
    for k in range(panels):
        pc1[band, k] = sums[k]
    c1_copies = rim_push(c1, REACH)
    pc1_copies = axis_push(pc1, "band", band, n_band)
    pending += v1_copies + c1_copies + pc1_copies

    lane = lax.broadcasted_iota(jnp.int32, (maps, 128), 1)

    def packed(parts):
        out = jnp.zeros((maps, 128), F32)
        for at, part in enumerate(parts):
            out = jnp.where(lane == at, jnp.sum(part, axis=1, keepdims=True), out)
        return out

    def total_of(buf, count):
        out = buf[0]
        for k in range(1, count):
            out = out + buf[k]
        return out

    red_lon[0, lon] = packed([rr, pw, ww])
    lon_copies = axis_push(red_lon.at[0], "lon", lon, n_lon)
    pending += lon_copies

    def split_value(j, carry):
        hi, lo = halves(v1[j])
        vs[j, pl.ds(0, maps)] = hi
        vs[j, pl.ds(maps, maps)] = lo
        return carry

    def second_near(i, carry):
        w2[i] = noise_ref[pl.ds(i, 1)] * v1[DEPTH + i] + near_product(i)
        return carry

    lax.fori_loop(DEPTH, leaves + DEPTH, split_value, 0)

    def second_near_pair(g, carry):
        second_near(DEPTH + 2 * g, carry)
        second_near(DEPTH + 2 * g + 1, carry)
        return carry

    lax.fori_loop(0, (leaves - 2 * DEPTH) // 2, second_near_pair, 0)
    landed(lon_copies)
    red_band[0, band] = total_of(red_lon.at[0], n_lon)
    band_copies = axis_push(red_band.at[0], "band", band, n_band)
    pending += band_copies
    landed(v1_copies)
    for j in list(range(DEPTH)) + list(range(leaves + DEPTH, leaves + 2 * DEPTH)):
        split_value(j, 0)
    for i in list(range(DEPTH)) + list(range(leaves - DEPTH, leaves)):
        second_near(i, 0)
    landed(c1_copies + pc1_copies)
    panel_far(pc1)

    landed(band_copies)
    first_sums = total_of(red_band.at[0], n_band)
    rr0, pw0, ww0 = first_sums[:, 0:1], first_sums[:, 1:2], first_sums[:, 2:3]
    step0 = rr0 / pw0
    ratio = (rr0 - 2.0 * step0 * pw0 + step0 * step0 * ww0) / rr0

    def second_far(g, carry):
        rr, pw = carry
        for u in range(GROUP):
            i = g * GROUP + u
            w = w2[i] + far(i, c1)
            p, image = sky_ref[i], v1[DEPTH + i]
            residual = p - step0 * image
            direction = residual + ratio * p
            image = (image - step0 * w) + ratio * image
            sol_ref[i] = direction
            res_ref[i] = residual
            w2[i] = image
            rr, pw = rr + residual * residual, pw + direction * image
        return rr, pw

    rr, pw = lax.fori_loop(0, leaves // GROUP, second_far, (zero, zero))
    red_lon[1, lon] = packed([rr, pw])
    lon_copies = axis_push(red_lon.at[1], "lon", lon, n_lon)
    landed(lon_copies)
    red_band[1, band] = total_of(red_lon.at[1], n_lon)
    band_copies = axis_push(red_band.at[1], "band", band, n_band)
    landed(band_copies)
    pending += lon_copies + band_copies
    second_sums = total_of(red_band.at[1], n_band)
    step1 = second_sums[:, 0:1] / second_sums[:, 1:2]

    def finish(i, carry):
        sol_ref[i] = step0 * sky_ref[i] + step1 * sol_ref[i]
        res_ref[i] = res_ref[i] - step1 * w2[i]
        return carry

    lax.fori_loop(0, leaves, finish, 0)
    for copy in pending:
        copy.wait_send()


def on_device(
    sky_maps,
    noise_var,
    position,
    leaf_basis,
    leaf_couple,
    transfer,
    panel_couple,
    near_list,
    far_list,
    panel_list,
    leaf_panel,
):
    n_lon = lax.axis_size("lon")
    n_band = lax.axis_size("band")
    maps, leaves, pixels = sky_maps.shape
    rank = leaf_basis.shape[2]
    panels = panel_couple.shape[0]
    slots = far_list.shape[1]
    pslots = panel_list.shape[1]
    span = 2 * DEPTH + 1
    count = 4 * 2 + 2 * 2 + 4 * (n_band - 1) + 2 * (n_lon - 1)
    vmem = pl.BlockSpec(memory_space=pltpu.VMEM)
    smem = pl.BlockSpec(memory_space=pltpu.SMEM)
    field = jnp.transpose(sky_maps, (1, 0, 2))
    rows = jnp.pad(jnp.transpose(position, (1, 0, 2)), ((0, 0), (0, 5), (0, 0)))
    shape = jax.ShapeDtypeStruct((leaves, maps, pixels), F32)
    sol, res = pl.pallas_call(
        functools.partial(kernel, leaves * n_lon, n_lon, n_band),
        out_shape=(shape, shape),
        in_specs=[vmem] * 7 + [smem] * 4,
        out_specs=(vmem, vmem),
        scratch_shapes=[
            pltpu.VMEM((leaves + 2 * DEPTH, 8, pixels), F32),
            pltpu.VMEM((leaves + 2 * DEPTH, pixels, 8), F32),
            pltpu.VMEM((leaves + 2 * DEPTH, maps, pixels), F32),
            pltpu.VMEM((leaves + 2 * DEPTH, maps, pixels), F32),
            pltpu.VMEM((leaves, maps, pixels), F32),
            pltpu.VMEM((leaves + 2 * REACH, maps, rank), F32),
            pltpu.VMEM((leaves + 2 * REACH, maps, rank), F32),
            pltpu.VMEM((n_band, panels, maps, rank), F32),
            pltpu.VMEM((n_band, panels, maps, rank), F32),
            pltpu.VMEM((panels, maps, rank), F32),
            pltpu.VMEM((leaves + 2 * DEPTH, 2 * maps, pixels), BF16),
            pltpu.VMEM((leaves, span * pixels, pixels), BF16),
            pltpu.VMEM((leaves, span * pixels, pixels), BF16),
            pltpu.VMEM((leaves, pixels, rank), BF16),
            pltpu.VMEM((leaves, pixels, rank), BF16),
            pltpu.VMEM((leaves, slots, rank, rank), BF16),
            pltpu.VMEM((leaves, slots, rank, rank), BF16),
            pltpu.VMEM((leaves, rank, rank), BF16),
            pltpu.VMEM((leaves, rank, rank), BF16),
            pltpu.VMEM((panels, pslots, rank, rank), BF16),
            pltpu.VMEM((panels, pslots, rank, rank), BF16),
            pltpu.VMEM((2, n_lon, maps, 128), F32),
            pltpu.VMEM((2, n_band, maps, 128), F32),
            pltpu.SemaphoreType.DMA((count,)),
            pltpu.SemaphoreType.DMA((count,)),
        ],
        compiler_params=pltpu.CompilerParams(
            collective_id=0, has_side_effects=True, vmem_limit_bytes=56 * 1024 * 1024
        ),
        cost_estimate=pl.CostEstimate(
            flops=4 * leaves * span * pixels * pixels * maps,
            bytes_accessed=8 * 1024 * 1024,
            transcendentals=2 * leaves * span * pixels * pixels,
        ),
    )(
        rows,
        field,
        noise_var,
        leaf_basis,
        leaf_couple,
        transfer,
        panel_couple,
        near_list,
        far_list,
        panel_list,
        leaf_panel[None],
    )
    return (jnp.transpose(sol, (1, 0, 2)), jnp.transpose(res, (1, 0, 2)))


def solution(mesh):
    placed = (
        P(None, ("band", "lon"), None),
        P(("band", "lon"), None),
        P(None, ("band", "lon"), None),
        P(("band", "lon"), None, None),
        P(("band", "lon"), None, None, None),
        P(("band", "lon"), None, None),
        P(("band", "lon"), None, None, None),
        P(("band", "lon"), None),
        P(("band", "lon"), None),
        P(("band", "lon"), None),
        P(("band", "lon")),
    )
    return jax.shard_map(
        on_device,
        mesh=mesh,
        in_specs=placed,
        out_specs=(P(None, ("band", "lon"), None), P(None, ("band", "lon"), None)),
        check_vma=False,
    )
```

time: 342 us -> 75.3 us (0.22)
  blocking collectives: 134 us -> 0 us
  matrix products: 63.6 us -> 0 us
  Pallas kernels: 0 us -> 61.5 us
  local copies, waits for them, and re-layouts: 68.4 us -> 12.8 us
  other arithmetic: 55 us -> 0 us
  starting transfers between devices: 11.7 us -> 0 us
  waiting for transfers between devices: 3.56 us -> 0 us
    psum x3 -> x0, blocking collectives: 116 us -> none  [the longest x2 79.5 us: square_total(): return lax.psum(jnp.sum(vector * vector, axis=(1, 2)), ('band', 'lon'))]
    dot_general x18 -> x0, matrix products: 63.6 us -> none  [the longest x2 42.9 us: on_device(): jnp.einsum('lspq,mlsq->mlp', near_blocks, rim_values[:, near_rows], preci...]
    pallas_call x0 -> x1, Pallas kernels: none -> 61.5 us  [on_device(): pl.pallas_call(functools.partial(kernel, leaves * n_lon, n_lon, n_band),...]
    dynamic_update_slice x16 -> x0, other arithmetic: 45.2 us -> none  [on_device(): lax.map(leaf_blocks, (jnp.transpose(position, (1, 0, 2)), near_rows, near...]
    slice x33 -> x0, local copies, waits for them, and re-layouts: 22.8 us -> none  [the longest x16 22 us: matern_block(): rows_pos[component][None, :, None] - cols_pos[component][:, None, :]]
    mul x16 -> x0, local copies, waits for them, and re-layouts: 20 us -> none  [leaf_blocks(): matern_block(rows_pos, cols_pos, length_scale) * slot_mask[:, None, None]]
    gather x22 -> x0, local copies, waits for them, and re-layouts: 18.5 us -> none  [the longest x16 9.14 us: leaf_blocks(): cols_pos = rim_pos[:, rows_index]]
    all_gather x2 -> x0, blocking collectives: 17.7 us -> none  [on_device(): band_coeffs = lax.all_gather(panel_coeffs, 'band', axis=1, tiled=True)]
  transfers between devices with their start and end apart: 6 -> 0, of which waited for: 1 -> 0; matrix products, arithmetic and copies ran while one was open for 33% -> 0% of each run, Pallas kernels for 0% -> 0%
where the time goes in v1:
time: 75.3 us; the launch traced here: 74.9 us
  Pallas kernels  61.5 us (82%)
  local copies, waits for them, and re-layouts  12.8 us (17%)
    pallas_call x1, Pallas kernels, on_device(): pl.pallas_call(functools.partial(kernel, leaves * n_lon, n_lon, n_band),...  61.5 us
    unnamed x7, local copies, waits for them, and re-layouts  12.1 us

profile of v1, /device:TPU:0, one launch (start us, length us, event | category | flops | bytes accessed | tf_op | source)
XLA Modules:
  0.0 74.9 jit_solution(4890291385501429822)
XLA Ops:
  0.6 1.4 %copy.16.near_ref = s32[16,5]{1,0:T(8,128)} copy(s32[16,5]{0,1:T(8,128)} %param.18) | data formatting | bytes 640 | tf_op args[7]
  2.0 1.3 %copy.17.far_ref = s32[16,4]{1,0:T(8,128)} copy(s32[16,4]{0,1:T(4,128)} %param.19) | data formatting | bytes 512 | tf_op args[8]
  3.3 0.8 %copy.23 = f32[3,16,256]{2,0,1:T(4,128)S(1)} copy(f32[3,16,256]{2,1,0:T(8,128)} %param.13) | data formatting | bytes 98304 | tf_op args[2]
  4.2 0.7 pad.4.pos_ref
  4.8 1.8 %copy.22 = f32[16,16,256]{2,0,1:T(8,128)} copy(f32[16,16,256]{2,1,0:T(8,128)} %param.11) | data formatting | bytes 524288 | tf_op args[0]
  6.6 3.2 %copy.15.basis_ref = f32[16,256,64]{2,1,0:T(8,128)} copy(f32[16,256,64]{1,2,0:T(8,128)} %param.14) | data formatting | bytes 2097152 | tf_op args[3]
  9.8 61.5 %shard_map.122 = (f32[16,16,256]{2,1,0:T(8,128)}, f32[16,16,256]{2,1,0:T(8,128)}) custom-call(f32[16,8,256]{2,1,0:T(8,128)} %pad.4.pos_ref, f32[16,16,256]{2,1,0:T(8,128)} %bitcast.12, f32[16,256]{1,0:T(8,128)} %noise_ref.1, f32[16,256,64]{2,1,0:T(8,128)} %copy.15.basis_ref, f32[16,4,64,64]{3,2,1,0:T(8,128)} %couple_ref.1, f32[16,64,64]{2,1,0:T(8,128)} %transfer_ref.1, ...), custom_call_target="tpu_custom_call" | custom-call | flops 335544320 | bytes 8388608 | tf_op jit(solution)/shard_map/pallas_call | solution.py:394
  71.3 1.8 %copy.18 = f32[16,16,256]{2,1,0:T(8,128)} copy(f32[16,16,256]{2,0,1:T(8,128)} %bitcast.11) | data formatting | bytes 524288
  73.1 1.8 %copy.19 = f32[16,16,256]{2,1,0:T(8,128)} copy(f32[16,16,256]{2,0,1:T(8,128)} %bitcast.10) | data formatting | bytes 524288

commit v2 on v1

--- a/solution.py
+++ b/solution.py
@@ -16,7 +16,7 @@
 NN = (((1,), (0,)), ((), ()))
 NT = (((1,), (1,)), ((), ()))
 MESH = pl.DeviceIdType.MESH
-GROUP = 4
+GROUP = 8
 
 
 def halves(x):
@@ -57,6 +57,8 @@
     v0,
     v1,
     w2,
+    dirs,
+    resid,
     c0,
     c1,
     pc0,
@@ -78,11 +80,11 @@
     send_sem,
     recv_sem,
 ):
-    leaves, maps, pixels = sky_ref.shape
-    rank = basis_ref.shape[2]
+    maps, leaves, pixels = sky_ref.shape
+    rank = basis_ref.shape[1]
     panels = pcouple_ref.shape[0]
-    slots = far_ref.shape[1]
-    near_slots = near_ref.shape[1]
+    slots = far_ref.shape[0]
+    near_slots = near_ref.shape[0]
     lon = lax.axis_index("lon")
     band = lax.axis_index("band")
     right = lax.rem(lon + 1, n_lon)
@@ -134,8 +136,11 @@
         pl.semaphore_signal(
             barrier, inc=1, device_id={"band": lax.rem(band + k, n_band)}, device_id_type=MESH
         )
-    posx[pl.ds(DEPTH, leaves)] = pos_ref[...]
-    v0[pl.ds(DEPTH, leaves)] = sky_ref[...]
+    posx[pl.ds(DEPTH, leaves)] = jnp.zeros((leaves,) + posx.shape[1:], F32)
+    for i in range(leaves):
+        v0[DEPTH + i] = sky_ref[:, i, :]
+        for component in range(3):
+            posx[DEPTH + i, component : component + 1] = pos_ref[component, i : i + 1]
     pl.semaphore_wait(barrier, n_lon - 1 + n_band - 1)
     pos_copies = rim_push(posx, DEPTH)
     v0_copies = rim_push(v0, DEPTH)
@@ -147,22 +152,24 @@
         for s in range(slots):
             whi[i, s], wlo[i, s] = halves(couple_ref[i, s])
 
-    def upward(i, value, cx, sums):
-        c = dot3(value, bhi[i], blo[i], NN)
-        cx[REACH + i] = c
-        up = dot3(c, thi[i], tlo[i], NN)
-        home = home_ref[0, i]
-        return [sums[k] + up * jnp.where(home == k, 1.0, 0.0).astype(F32) for k in range(panels)]
+    def upward(g, values, cx, sums):
+        ids = [g * GROUP + u for u in range(GROUP)]
+        cs = [dot3(values[u], bhi[i], blo[i], NT) for u, i in enumerate(ids)]
+        ups = [dot3(cs[u], thi[i], tlo[i], NN) for u, i in enumerate(ids)]
+        for u, i in enumerate(ids):
+            cx[REACH + i] = cs[u]
+            sums = [
+                sums[k] + ups[u] * jnp.where(home_ref[0, i] == k, 1.0, 0.0).astype(F32)
+                for k in range(panels)
+            ]
+        return sums
 
     zero_panels = [jnp.zeros((maps, rank), F32) for _ in range(panels)]
 
     def first_coeffs(g, sums):
         for u in range(GROUP):
             prepare(g * GROUP + u)
-        for u in range(GROUP):
-            i = g * GROUP + u
-            sums = upward(i, sky_ref[i], c0, sums)
-        return sums
+        return upward(g, [v0[DEPTH + g * GROUP + u] for u in range(GROUP)], c0, sums)
 
     sums = lax.fori_loop(0, leaves // GROUP, first_coeffs, zero_panels)
     for k in range(panels):
@@ -175,12 +182,11 @@
             ghi[k, s], glo[k, s] = halves(pcouple_ref[k, s])
 
     landed(pos_copies + v0_copies)
-    scale = math.sqrt(3.0) / (2.0 * math.pi / cycle)
+    log2e = 1.0 / math.log(2.0)
+    scale = log2e * math.sqrt(3.0) / (2.0 * math.pi / cycle)
 
     def columns(j, carry):
-        scaled = posx[j] * scale
-        posx_scaled = scaled
-        posc[j] = jnp.transpose(posx_scaled)
+        posc[j] = jnp.transpose(posx[j] * scale)
         hi, lo = halves(v0[j])
         vs[j, pl.ds(0, maps)] = hi
         vs[j, pl.ds(maps, maps)] = lo
@@ -198,7 +204,8 @@
 
     def first_near(i, carry):
         rows = posx[DEPTH + i] * scale
-        me = near_ref[i, 0]
+        me = near_ref[0, i]
+        total = noise_ref[pl.ds(i, 1)] * v0[DEPTH + i]
         for d in range(2 * DEPTH + 1):
             offset = d - DEPTH
             if offset == 0:
@@ -206,10 +213,11 @@
             else:
                 weight = jnp.asarray(0.0, F32)
                 for s in range(1, near_slots):
-                    other = near_ref[i, s]
+                    other = near_ref[s, i]
                     gap = other - me
                     hit = (gap == offset) | (gap == offset - cycle) | (gap == offset + cycle)
                     weight = weight + jnp.where((other >= 0) & hit, AMPLITUDE, 0.0).astype(F32)
+            slope = weight * math.log(2.0)
             for q in range(0, pixels, chunk):
                 squared = None
                 for component in range(3):
@@ -219,11 +227,16 @@
                     )
                     squared = gap * gap if squared is None else squared + gap * gap
                 t = squared * lax.rsqrt(jnp.maximum(squared, 1e-30))
-                block = (weight + weight * t) * jnp.exp(-t)
+                block = (weight + slope * t) * jnp.exp2(-t)
                 hi, lo = halves(block)
                 khi[i, pl.ds(d * pixels + q, chunk)] = hi
                 klo[i, pl.ds(d * pixels + q, chunk)] = lo
-        v1[DEPTH + i] = noise_ref[pl.ds(i, 1)] * sky_ref[i] + near_product(i)
+            values = vs[i + d]
+            at = pl.ds(d * pixels, pixels)
+            both = lax.dot_general(values, khi[i, at], NN, preferred_element_type=F32)
+            rest = lax.dot_general(values[:maps], klo[i, at], NN, preferred_element_type=F32)
+            total = total + (both[:maps] + both[maps:] + rest)
+        v1[DEPTH + i] = total
         return carry
 
     lax.fori_loop(0, leaves, first_near, 0)
@@ -239,12 +252,12 @@
     def far(i, cx):
         total = dot3(pf[home_ref[0, i]], thi[i], tlo[i], NT)
         for s in range(slots):
-            gap = far_ref[i, s] - (first + i)
+            gap = far_ref[s, i] - (first + i)
             gap = jnp.where(gap > REACH, gap - cycle, gap)
             gap = jnp.where(gap < -REACH, gap + cycle, gap)
             row = jnp.clip(i + REACH + gap, 0, leaves + 2 * REACH - 1)
             total = total + dot3(cx[row], whi[i, s], wlo[i, s], NT)
-        return dot3(total, bhi[i], blo[i], NT)
+        return dot3(total, bhi[i], blo[i], NN)
 
     landed(c0_copies + pc0_copies)
     panel_far(pc0)
@@ -252,16 +265,14 @@
 
     def first_far(g, carry):
         sums, rr, pw, ww = carry
-        out = []
+        fars = [far(g * GROUP + u, c0) for u in range(GROUP)]
+        out = [v1[DEPTH + g * GROUP + u] + fars[u] for u in range(GROUP)]
+        sums = upward(g, out, c1, sums)
         for u in range(GROUP):
             i = g * GROUP + u
-            w = v1[DEPTH + i] + far(i, c0)
+            p, w = v0[DEPTH + i], out[u]
             v1[DEPTH + i] = w
-            p = sky_ref[i]
             rr, pw, ww = rr + p * p, pw + p * w, ww + w * w
-            out.append(w)
-        for u in range(GROUP):
-            sums = upward(g * GROUP + u, out[u], c1, sums)
         return sums, rr, pw, ww
 
     sums, rr, pw, ww = lax.fori_loop(
@@ -304,12 +315,14 @@
 
     lax.fori_loop(DEPTH, leaves + DEPTH, split_value, 0)
 
-    def second_near_pair(g, carry):
-        second_near(DEPTH + 2 * g, carry)
-        second_near(DEPTH + 2 * g + 1, carry)
+    batch = 2 * DEPTH
+
+    def second_near_batch(g, carry):
+        for u in range(batch):
+            second_near(DEPTH + batch * g + u, carry)
         return carry
 
-    lax.fori_loop(0, (leaves - 2 * DEPTH) // 2, second_near_pair, 0)
+    lax.fori_loop(0, (leaves - 2 * DEPTH) // batch, second_near_batch, 0)
     landed(lon_copies)
     red_band[0, band] = total_of(red_lon.at[0], n_lon)
     band_copies = axis_push(red_band.at[0], "band", band, n_band)
@@ -330,15 +343,16 @@
 
     def second_far(g, carry):
         rr, pw = carry
+        fars = [far(g * GROUP + u, c1) for u in range(GROUP)]
         for u in range(GROUP):
             i = g * GROUP + u
-            w = w2[i] + far(i, c1)
-            p, image = sky_ref[i], v1[DEPTH + i]
+            w = w2[i] + fars[u]
+            p, image = v0[DEPTH + i], v1[DEPTH + i]
             residual = p - step0 * image
             direction = residual + ratio * p
             image = (image - step0 * w) + ratio * image
-            sol_ref[i] = direction
-            res_ref[i] = residual
+            dirs[i] = direction
+            resid[i] = residual
             w2[i] = image
             rr, pw = rr + residual * residual, pw + direction * image
         return rr, pw
@@ -354,12 +368,9 @@
     second_sums = total_of(red_band.at[1], n_band)
     step1 = second_sums[:, 0:1] / second_sums[:, 1:2]
 
-    def finish(i, carry):
-        sol_ref[i] = step0 * sky_ref[i] + step1 * sol_ref[i]
-        res_ref[i] = res_ref[i] - step1 * w2[i]
-        return carry
-
-    lax.fori_loop(0, leaves, finish, 0)
+    for i in range(leaves):
+        sol_ref[:, i, :] = step0 * v0[DEPTH + i] + step1 * dirs[i]
+        res_ref[:, i, :] = resid[i] - step1 * w2[i]
     for copy in pending:
         copy.wait_send()
 
@@ -388,9 +399,7 @@
     count = 4 * 2 + 2 * 2 + 4 * (n_band - 1) + 2 * (n_lon - 1)
     vmem = pl.BlockSpec(memory_space=pltpu.VMEM)
     smem = pl.BlockSpec(memory_space=pltpu.SMEM)
-    field = jnp.transpose(sky_maps, (1, 0, 2))
-    rows = jnp.pad(jnp.transpose(position, (1, 0, 2)), ((0, 0), (0, 5), (0, 0)))
-    shape = jax.ShapeDtypeStruct((leaves, maps, pixels), F32)
+    shape = jax.ShapeDtypeStruct((maps, leaves, pixels), F32)
     sol, res = pl.pallas_call(
         functools.partial(kernel, leaves * n_lon, n_lon, n_band),
         out_shape=(shape, shape),
@@ -402,6 +411,8 @@
             pltpu.VMEM((leaves + 2 * DEPTH, maps, pixels), F32),
             pltpu.VMEM((leaves + 2 * DEPTH, maps, pixels), F32),
             pltpu.VMEM((leaves, maps, pixels), F32),
+            pltpu.VMEM((leaves, maps, pixels), F32),
+            pltpu.VMEM((leaves, maps, pixels), F32),
             pltpu.VMEM((leaves + 2 * REACH, maps, rank), F32),
             pltpu.VMEM((leaves + 2 * REACH, maps, rank), F32),
             pltpu.VMEM((n_band, panels, maps, rank), F32),
@@ -410,8 +421,8 @@
             pltpu.VMEM((leaves + 2 * DEPTH, 2 * maps, pixels), BF16),
             pltpu.VMEM((leaves, span * pixels, pixels), BF16),
             pltpu.VMEM((leaves, span * pixels, pixels), BF16),
-            pltpu.VMEM((leaves, pixels, rank), BF16),
-            pltpu.VMEM((leaves, pixels, rank), BF16),
+            pltpu.VMEM((leaves, rank, pixels), BF16),
+            pltpu.VMEM((leaves, rank, pixels), BF16),
             pltpu.VMEM((leaves, slots, rank, rank), BF16),
             pltpu.VMEM((leaves, slots, rank, rank), BF16),
             pltpu.VMEM((leaves, rank, rank), BF16),
@@ -432,19 +443,19 @@
             transcendentals=2 * leaves * span * pixels * pixels,
         ),
     )(
-        rows,
-        field,
+        position,
+        sky_maps,
         noise_var,
-        leaf_basis,
+        jnp.swapaxes(leaf_basis, 1, 2),
         leaf_couple,
         transfer,
         panel_couple,
-        near_list,
-        far_list,
+        near_list.T,
+        far_list.T,
         panel_list,
         leaf_panel[None],
     )
-    return (jnp.transpose(sol, (1, 0, 2)), jnp.transpose(res, (1, 0, 2)))
+    return (sol, res)
 
 
 def solution(mesh):

time: 75.3 us -> 61 us (0.81)
  local copies, waits for them, and re-layouts: 12.8 us -> 3.34 us
  Pallas kernels: 61.5 us -> 56.8 us
    unnamed x7 -> x2, local copies, waits for them, and re-layouts: 12.1 us -> 3.34 us
    pallas_call x1, Pallas kernels: 61.5 us -> 56.8 us  [on_device(): pl.pallas_call(functools.partial(kernel, leaves * n_lon, n_lon, n_band),...]
where the time goes in v2:
time: 61 us; the launch traced here: 60.8 us
  Pallas kernels  56.8 us (93%)
  local copies, waits for them, and re-layouts  3.34 us (5%)
  between operations  0.64 us (1%)
    pallas_call x1, Pallas kernels, on_device(): pl.pallas_call(functools.partial(kernel, leaves * n_lon, n_lon, n_band),...  56.8 us
    unnamed x2, local copies, waits for them, and re-layouts  3.34 us

profile of v2, /device:TPU:0, one launch (start us, length us, event | category | flops | bytes accessed | tf_op | source)
XLA Modules:
  0.0 60.8 jit_solution(7538564348382511340)
XLA Ops:
  0.6 56.8 %shard_map.122 = (f32[16,16,256]{2,1,0:T(8,128)}, f32[16,16,256]{2,1,0:T(8,128)}) custom-call(f32[3,16,256]{2,1,0:T(8,128)} %pos_ref.1, f32[16,16,256]{2,1,0:T(8,128)} %sky_ref.1, f32[16,256]{1,0:T(8,128)} %noise_ref.1, f32[16,64,256]{2,1,0:T(8,128)} %bitcast.4, f32[16,4,64,64]{3,2,1,0:T(8,128)} %couple_ref.1, f32[16,64,64]{2,1,0:T(8,128)} %transfer_ref.1, ...), custom_call_target="tpu_custom_call" | custom-call | flops 335544320 | bytes 8388608 | tf_op jit(solution)/shard_map/pallas_call | solution.py:403
  57.5 1.7 %copy.15 = f32[16,16,256]{2,1,0:T(8,128)} copy(f32[16,16,256]{2,1,0:T(8,128)} %get-tuple-element.4) | data formatting | bytes 524288
  59.1 1.7 %copy.16 = f32[16,16,256]{2,1,0:T(8,128)} copy(f32[16,16,256]{2,1,0:T(8,128)} %get-tuple-element.5) | data formatting | bytes 524288

commit v3 on v2

--- a/solution.py
+++ b/solution.py
@@ -33,6 +33,18 @@
     )
     rest = lax.dot_general(hi, blo, dims, preferred_element_type=F32)
     return both[:n] + both[n:] + rest
+
+
+def spread(a, bcat):
+    hi, lo = halves(a)
+    return lax.dot_general(
+        jnp.concatenate([hi, lo], axis=0), bcat, NT, preferred_element_type=F32
+    )
+
+
+def gathered(r):
+    n, k = r.shape[0] // 2, r.shape[1] // 2
+    return r[:n, :k] + r[n:, :k] + r[:n, k:]
 
 
 def kernel(
@@ -53,7 +65,8 @@
     sol_ref,
     res_ref,
     posx,
-    posc,
+    posa,
+    posb,
     v0,
     v1,
     w2,
@@ -67,12 +80,9 @@
     vs,
     khi,
     klo,
-    bhi,
-    blo,
-    whi,
-    wlo,
-    thi,
-    tlo,
+    bcat,
+    wcat,
+    tcat,
     ghi,
     glo,
     red_lon,
@@ -147,15 +157,19 @@
     pending += pos_copies + v0_copies
 
     def prepare(i):
-        bhi[i], blo[i] = halves(basis_ref[i])
-        thi[i], tlo[i] = halves(transfer_ref[i])
+        top, low = pl.ds(0, rank), pl.ds(rank, rank)
+        bcat[i, top], bcat[i, low] = halves(basis_ref[i])
+        tcat[i, top], tcat[i, low] = halves(transfer_ref[i])
         for s in range(slots):
-            whi[i, s], wlo[i, s] = halves(couple_ref[i, s])
+            wcat[i, s, top], wcat[i, s, low] = halves(couple_ref[i, s])
 
     def upward(g, values, cx, sums):
         ids = [g * GROUP + u for u in range(GROUP)]
-        cs = [dot3(values[u], bhi[i], blo[i], NT) for u, i in enumerate(ids)]
-        ups = [dot3(cs[u], thi[i], tlo[i], NN) for u, i in enumerate(ids)]
+        cs = [gathered(spread(values[u], bcat[i])) for u, i in enumerate(ids)]
+        ups = [
+            dot3(cs[u], tcat[i, pl.ds(0, rank)], tcat[i, pl.ds(rank, rank)], NN)
+            for u, i in enumerate(ids)
+        ]
         for u, i in enumerate(ids):
             cx[REACH + i] = cs[u]
             sums = [
@@ -185,8 +199,28 @@
     log2e = 1.0 / math.log(2.0)
     scale = log2e * math.sqrt(3.0) / (2.0 * math.pi / cycle)
 
+    middle = posx[DEPTH + leaves // 2, :, 0:1]
+    ones = jnp.ones((1, pixels), F32)
+    spare = jnp.zeros((8, pixels), F32)
+
+    def thirds(x):
+        one = x.astype(BF16).astype(F32)
+        two = (x - one).astype(BF16).astype(F32)
+        return one, two, (x - one) - two
+
     def columns(j, carry):
-        posc[j] = jnp.transpose(posx[j] * scale)
+        place = ((posx[j] - middle) * scale)[:3]
+        one, two, three = thirds(place)
+        norms = thirds(jnp.sum(place * place, axis=0, keepdims=True))
+        target = [one, one, two, one, three, two]
+        source = [one, two, one, three, one, two]
+        posa[j] = jnp.concatenate(
+            target + list(norms) + [ones] * 3 + [spare], axis=0
+        ).astype(BF16)
+        source = [-2.0 * x for x in source]
+        posb[j] = jnp.transpose(
+            jnp.concatenate(source + [ones] * 3 + list(norms) + [spare], axis=0)
+        ).astype(BF16)
         hi, lo = halves(v0[j])
         vs[j, pl.ds(0, maps)] = hi
         vs[j, pl.ds(maps, maps)] = lo
@@ -200,10 +234,10 @@
         rest = lax.dot_general(values[:maps], klo[i], NN, preferred_element_type=F32)
         return both[:maps] + both[maps:] + rest
 
-    chunk = 64
+    chunk = 128
 
     def first_near(i, carry):
-        rows = posx[DEPTH + i] * scale
+        rows = posa[DEPTH + i]
         me = near_ref[0, i]
         total = noise_ref[pl.ds(i, 1)] * v0[DEPTH + i]
         for d in range(2 * DEPTH + 1):
@@ -219,14 +253,11 @@
                     weight = weight + jnp.where((other >= 0) & hit, AMPLITUDE, 0.0).astype(F32)
             slope = weight * math.log(2.0)
             for q in range(0, pixels, chunk):
-                squared = None
-                for component in range(3):
-                    gap = (
-                        posc[i + d, pl.ds(q, chunk), component : component + 1]
-                        - rows[component : component + 1]
-                    )
-                    squared = gap * gap if squared is None else squared + gap * gap
-                t = squared * lax.rsqrt(jnp.maximum(squared, 1e-30))
+                squared = lax.dot_general(
+                    posb[i + d, pl.ds(q, chunk)], rows, NN, preferred_element_type=F32
+                )
+                squared = jnp.maximum(squared, 1e-30)
+                t = squared * lax.rsqrt(squared)
                 block = (weight + slope * t) * jnp.exp2(-t)
                 hi, lo = halves(block)
                 khi[i, pl.ds(d * pixels + q, chunk)] = hi
@@ -250,14 +281,16 @@
             pf[k] = total
 
     def far(i, cx):
-        total = dot3(pf[home_ref[0, i]], thi[i], tlo[i], NT)
+        total = spread(pf[home_ref[0, i]], tcat[i])
         for s in range(slots):
             gap = far_ref[s, i] - (first + i)
             gap = jnp.where(gap > REACH, gap - cycle, gap)
             gap = jnp.where(gap < -REACH, gap + cycle, gap)
             row = jnp.clip(i + REACH + gap, 0, leaves + 2 * REACH - 1)
-            total = total + dot3(cx[row], whi[i, s], wlo[i, s], NT)
-        return dot3(total, bhi[i], blo[i], NN)
+            total = total + spread(cx[row], wcat[i, s])
+        return dot3(
+            gathered(total), bcat[i, pl.ds(0, rank)], bcat[i, pl.ds(rank, rank)], NN
+        )
 
     landed(c0_copies + pc0_copies)
     panel_far(pc0)
@@ -407,7 +440,8 @@
         out_specs=(vmem, vmem),
         scratch_shapes=[
             pltpu.VMEM((leaves + 2 * DEPTH, 8, pixels), F32),
-            pltpu.VMEM((leaves + 2 * DEPTH, pixels, 8), F32),
+            pltpu.VMEM((leaves + 2 * DEPTH, 32, pixels), BF16),
+            pltpu.VMEM((leaves + 2 * DEPTH, pixels, 32), BF16),
             pltpu.VMEM((leaves + 2 * DEPTH, maps, pixels), F32),
             pltpu.VMEM((leaves + 2 * DEPTH, maps, pixels), F32),
             pltpu.VMEM((leaves, maps, pixels), F32),
@@ -421,12 +455,9 @@
             pltpu.VMEM((leaves + 2 * DEPTH, 2 * maps, pixels), BF16),
             pltpu.VMEM((leaves, span * pixels, pixels), BF16),
             pltpu.VMEM((leaves, span * pixels, pixels), BF16),
-            pltpu.VMEM((leaves, rank, pixels), BF16),
-            pltpu.VMEM((leaves, rank, pixels), BF16),
-            pltpu.VMEM((leaves, slots, rank, rank), BF16),
-            pltpu.VMEM((leaves, slots, rank, rank), BF16),
-            pltpu.VMEM((leaves, rank, rank), BF16),
-            pltpu.VMEM((leaves, rank, rank), BF16),
+            pltpu.VMEM((leaves, 2 * rank, pixels), BF16),
+            pltpu.VMEM((leaves, slots, 2 * rank, rank), BF16),
+            pltpu.VMEM((leaves, 2 * rank, rank), BF16),
             pltpu.VMEM((panels, pslots, rank, rank), BF16),
             pltpu.VMEM((panels, pslots, rank, rank), BF16),
             pltpu.VMEM((2, n_lon, maps, 128), F32),

time: 61 us -> 64.9 us (1.064)
  Pallas kernels: 56.8 us -> 60.7 us
    pallas_call x1, Pallas kernels: 56.8 us -> 60.7 us  [on_device(): pl.pallas_call(functools.partial(kernel, leaves * n_lon, n_lon, n_band),...]
where the time goes in v3:
time: 64.9 us; the launch traced here: 64.7 us
  Pallas kernels  60.7 us (94%)
  local copies, waits for them, and re-layouts  3.34 us (5%)
    pallas_call x1, Pallas kernels, on_device(): pl.pallas_call(functools.partial(kernel, leaves * n_lon, n_lon, n_band),...  60.7 us
    unnamed x2, local copies, waits for them, and re-layouts  3.34 us

profile of v3, /device:TPU:0, one launch (start us, length us, event | category | flops | bytes accessed | tf_op | source)
XLA Modules:
  0.0 64.7 jit_solution(363490868861487278)
XLA Ops:
  0.6 60.7 %shard_map.122 = (f32[16,16,256]{2,1,0:T(8,128)}, f32[16,16,256]{2,1,0:T(8,128)}) custom-call(f32[3,16,256]{2,1,0:T(8,128)} %pos_ref.1, f32[16,16,256]{2,1,0:T(8,128)} %sky_ref.1, f32[16,256]{1,0:T(8,128)} %noise_ref.1, f32[16,64,256]{2,1,0:T(8,128)} %bitcast.4, f32[16,4,64,64]{3,2,1,0:T(8,128)} %couple_ref.1, f32[16,64,64]{2,1,0:T(8,128)} %transfer_ref.1, ...), custom_call_target="tpu_custom_call" | custom-call | flops 335544320 | bytes 8388608 | tf_op jit(solution)/shard_map/pallas_call | solution.py:436
  61.3 1.7 %copy.15 = f32[16,16,256]{2,1,0:T(8,128)} copy(f32[16,16,256]{2,1,0:T(8,128)} %get-tuple-element.4) | data formatting | bytes 524288
  63.0 1.7 %copy.16 = f32[16,16,256]{2,1,0:T(8,128)} copy(f32[16,16,256]{2,1,0:T(8,128)} %get-tuple-element.5) | data formatting | bytes 524288

commit v4 on v2

--- a/solution.py
+++ b/solution.py
@@ -33,6 +33,18 @@
     )
     rest = lax.dot_general(hi, blo, dims, preferred_element_type=F32)
     return both[:n] + both[n:] + rest
+
+
+def spread(a, bcat):
+    hi, lo = halves(a)
+    return lax.dot_general(
+        jnp.concatenate([hi, lo], axis=0), bcat, NT, preferred_element_type=F32
+    )
+
+
+def gathered(r):
+    n, k = r.shape[0] // 2, r.shape[1] // 2
+    return r[:n, :k] + r[n:, :k] + r[:n, k:]
 
 
 def kernel(
@@ -67,12 +79,9 @@
     vs,
     khi,
     klo,
-    bhi,
-    blo,
-    whi,
-    wlo,
-    thi,
-    tlo,
+    bcat,
+    wcat,
+    tcat,
     ghi,
     glo,
     red_lon,
@@ -147,15 +156,19 @@
     pending += pos_copies + v0_copies
 
     def prepare(i):
-        bhi[i], blo[i] = halves(basis_ref[i])
-        thi[i], tlo[i] = halves(transfer_ref[i])
-        for s in range(slots):
-            whi[i, s], wlo[i, s] = halves(couple_ref[i, s])
+        top, low = pl.ds(0, rank), pl.ds(rank, rank)
+        bcat[i, top], bcat[i, low] = halves(basis_ref[i])
+        tcat[i, top], tcat[i, low] = halves(transfer_ref[i])
+        beside = jnp.concatenate([couple_ref[i, s] for s in range(slots)], axis=1)
+        wcat[i, top], wcat[i, low] = halves(beside)
 
     def upward(g, values, cx, sums):
         ids = [g * GROUP + u for u in range(GROUP)]
-        cs = [dot3(values[u], bhi[i], blo[i], NT) for u, i in enumerate(ids)]
-        ups = [dot3(cs[u], thi[i], tlo[i], NN) for u, i in enumerate(ids)]
+        cs = [gathered(spread(values[u], bcat[i])) for u, i in enumerate(ids)]
+        ups = [
+            dot3(cs[u], tcat[i, pl.ds(0, rank)], tcat[i, pl.ds(rank, rank)], NN)
+            for u, i in enumerate(ids)
+        ]
         for u, i in enumerate(ids):
             cx[REACH + i] = cs[u]
             sums = [
@@ -250,14 +263,18 @@
             pf[k] = total
 
     def far(i, cx):
-        total = dot3(pf[home_ref[0, i]], thi[i], tlo[i], NT)
+        total = spread(pf[home_ref[0, i]], tcat[i])
+        parts = []
         for s in range(slots):
             gap = far_ref[s, i] - (first + i)
             gap = jnp.where(gap > REACH, gap - cycle, gap)
             gap = jnp.where(gap < -REACH, gap + cycle, gap)
             row = jnp.clip(i + REACH + gap, 0, leaves + 2 * REACH - 1)
-            total = total + dot3(cx[row], whi[i, s], wlo[i, s], NT)
-        return dot3(total, bhi[i], blo[i], NN)
+            parts.append(cx[row])
+        total = total + spread(jnp.concatenate(parts, axis=1), wcat[i])
+        return dot3(
+            gathered(total), bcat[i, pl.ds(0, rank)], bcat[i, pl.ds(rank, rank)], NN
+        )
 
     landed(c0_copies + pc0_copies)
     panel_far(pc0)
@@ -421,12 +438,9 @@
             pltpu.VMEM((leaves + 2 * DEPTH, 2 * maps, pixels), BF16),
             pltpu.VMEM((leaves, span * pixels, pixels), BF16),
             pltpu.VMEM((leaves, span * pixels, pixels), BF16),
-            pltpu.VMEM((leaves, rank, pixels), BF16),
-            pltpu.VMEM((leaves, rank, pixels), BF16),
-            pltpu.VMEM((leaves, slots, rank, rank), BF16),
-            pltpu.VMEM((leaves, slots, rank, rank), BF16),
-            pltpu.VMEM((leaves, rank, rank), BF16),
-            pltpu.VMEM((leaves, rank, rank), BF16),
+            pltpu.VMEM((leaves, 2 * rank, pixels), BF16),
+            pltpu.VMEM((leaves, 2 * rank, slots * rank), BF16),
+            pltpu.VMEM((leaves, 2 * rank, rank), BF16),
             pltpu.VMEM((panels, pslots, rank, rank), BF16),
             pltpu.VMEM((panels, pslots, rank, rank), BF16),
             pltpu.VMEM((2, n_lon, maps, 128), F32),

time: 61 us -> 62 us (1.016)
  Pallas kernels: 56.8 us -> 57.8 us
    pallas_call x1, Pallas kernels: 56.8 us -> 57.8 us  [on_device(): pl.pallas_call(functools.partial(kernel, leaves * n_lon, n_lon, n_band),...]
where the time goes in v4:
time: 62 us; the launch traced here: 61.8 us
  Pallas kernels  57.8 us (93%)
  local copies, waits for them, and re-layouts  3.34 us (5%)
  between operations  0.64 us (1%)
    pallas_call x1, Pallas kernels, on_device(): pl.pallas_call(functools.partial(kernel, leaves * n_lon, n_lon, n_band),...  57.8 us
    unnamed x2, local copies, waits for them, and re-layouts  3.34 us

profile of v4, /device:TPU:0, one launch (start us, length us, event | category | flops | bytes accessed | tf_op | source)
XLA Modules:
  0.0 61.8 jit_solution(6385950612351947015)
XLA Ops:
  0.6 57.8 %shard_map.122 = (f32[16,16,256]{2,1,0:T(8,128)}, f32[16,16,256]{2,1,0:T(8,128)}) custom-call(f32[3,16,256]{2,1,0:T(8,128)} %pos_ref.1, f32[16,16,256]{2,1,0:T(8,128)} %sky_ref.1, f32[16,256]{1,0:T(8,128)} %noise_ref.1, f32[16,64,256]{2,1,0:T(8,128)} %bitcast.4, f32[16,4,64,64]{3,2,1,0:T(8,128)} %couple_ref.1, f32[16,64,64]{2,1,0:T(8,128)} %transfer_ref.1, ...), custom_call_target="tpu_custom_call" | custom-call | flops 335544320 | bytes 8388608 | tf_op jit(solution)/shard_map/pallas_call | solution.py:420
  58.5 1.7 %copy.15 = f32[16,16,256]{2,1,0:T(8,128)} copy(f32[16,16,256]{2,1,0:T(8,128)} %get-tuple-element.4) | data formatting | bytes 524288
  60.1 1.7 %copy.16 = f32[16,16,256]{2,1,0:T(8,128)} copy(f32[16,16,256]{2,1,0:T(8,128)} %get-tuple-element.5) | data formatting | bytes 524288

commit v5 on v2

--- a/solution.py
+++ b/solution.py
@@ -200,7 +200,7 @@
         rest = lax.dot_general(values[:maps], klo[i], NN, preferred_element_type=F32)
         return both[:maps] + both[maps:] + rest
 
-    chunk = 64
+    chunk = 32
 
     def first_near(i, carry):
         rows = posx[DEPTH + i] * scale

time: 61 us -> 61 us (level)
  no operation moved by 1% of the time
where the time goes in v5:
time: 61 us; the launch traced here: 60.8 us
  Pallas kernels  56.8 us (93%)
  local copies, waits for them, and re-layouts  3.34 us (5%)
  between operations  0.64 us (1%)
    pallas_call x1, Pallas kernels, on_device(): pl.pallas_call(functools.partial(kernel, leaves * n_lon, n_lon, n_band),...  56.8 us
    unnamed x2, local copies, waits for them, and re-layouts  3.34 us

profile of v5, /device:TPU:0, one launch (start us, length us, event | category | flops | bytes accessed | tf_op | source)
XLA Modules:
  0.0 60.8 jit_solution(6700419228883155615)
XLA Ops:
  0.6 56.8 %shard_map.122 = (f32[16,16,256]{2,1,0:T(8,128)}, f32[16,16,256]{2,1,0:T(8,128)}) custom-call(f32[3,16,256]{2,1,0:T(8,128)} %pos_ref.1, f32[16,16,256]{2,1,0:T(8,128)} %sky_ref.1, f32[16,256]{1,0:T(8,128)} %noise_ref.1, f32[16,64,256]{2,1,0:T(8,128)} %bitcast.4, f32[16,4,64,64]{3,2,1,0:T(8,128)} %couple_ref.1, f32[16,64,64]{2,1,0:T(8,128)} %transfer_ref.1, ...), custom_call_target="tpu_custom_call" | custom-call | flops 335544320 | bytes 8388608 | tf_op jit(solution)/shard_map/pallas_call | solution.py:403
  57.5 1.7 %copy.15 = f32[16,16,256]{2,1,0:T(8,128)} copy(f32[16,16,256]{2,1,0:T(8,128)} %get-tuple-element.4) | data formatting | bytes 524288
  59.1 1.7 %copy.16 = f32[16,16,256]{2,1,0:T(8,128)} copy(f32[16,16,256]{2,1,0:T(8,128)} %get-tuple-element.5) | data formatting | bytes 524288

commit v6 on v5

--- a/solution.py
+++ b/solution.py
@@ -186,7 +186,11 @@
     scale = log2e * math.sqrt(3.0) / (2.0 * math.pi / cycle)
 
     def columns(j, carry):
-        posc[j] = jnp.transpose(posx[j] * scale)
+        turned = jnp.transpose(posx[j] * scale)
+        for component in range(3):
+            posc[j, component] = jnp.broadcast_to(
+                turned[:, component : component + 1], (pixels, 128)
+            )
         hi, lo = halves(v0[j])
         vs[j, pl.ds(0, maps)] = hi
         vs[j, pl.ds(maps, maps)] = lo
@@ -219,18 +223,19 @@
                     weight = weight + jnp.where((other >= 0) & hit, AMPLITUDE, 0.0).astype(F32)
             slope = weight * math.log(2.0)
             for q in range(0, pixels, chunk):
-                squared = None
-                for component in range(3):
-                    gap = (
-                        posc[i + d, pl.ds(q, chunk), component : component + 1]
-                        - rows[component : component + 1]
-                    )
-                    squared = gap * gap if squared is None else squared + gap * gap
-                t = squared * lax.rsqrt(jnp.maximum(squared, 1e-30))
-                block = (weight + slope * t) * jnp.exp2(-t)
-                hi, lo = halves(block)
-                khi[i, pl.ds(d * pixels + q, chunk)] = hi
-                klo[i, pl.ds(d * pixels + q, chunk)] = lo
+                for p in range(0, pixels, 128):
+                    squared = None
+                    for component in range(3):
+                        gap = (
+                            posc[i + d, component, pl.ds(q, chunk)]
+                            - rows[component : component + 1, p : p + 128]
+                        )
+                        squared = gap * gap if squared is None else squared + gap * gap
+                    t = squared * lax.rsqrt(jnp.maximum(squared, 1e-30))
+                    block = (weight + slope * t) * jnp.exp2(-t)
+                    hi, lo = halves(block)
+                    khi[i, pl.ds(d * pixels + q, chunk), pl.ds(p, 128)] = hi
+                    klo[i, pl.ds(d * pixels + q, chunk), pl.ds(p, 128)] = lo
             values = vs[i + d]
             at = pl.ds(d * pixels, pixels)
             both = lax.dot_general(values, khi[i, at], NN, preferred_element_type=F32)
@@ -407,7 +412,7 @@
         out_specs=(vmem, vmem),
         scratch_shapes=[
             pltpu.VMEM((leaves + 2 * DEPTH, 8, pixels), F32),
-            pltpu.VMEM((leaves + 2 * DEPTH, pixels, 8), F32),
+            pltpu.VMEM((leaves + 2 * DEPTH, 3, pixels, 128), F32),
             pltpu.VMEM((leaves + 2 * DEPTH, maps, pixels), F32),
             pltpu.VMEM((leaves + 2 * DEPTH, maps, pixels), F32),
             pltpu.VMEM((leaves, maps, pixels), F32),

time: 61 us -> 66.4 us (1.089)
  Pallas kernels: 56.8 us -> 62.3 us
    pallas_call x1, Pallas kernels: 56.8 us -> 62.3 us  [on_device(): pl.pallas_call(functools.partial(kernel, leaves * n_lon, n_lon, n_band),...]
where the time goes in v6:
time: 66.4 us; the launch traced here: 66.3 us
  Pallas kernels  62.3 us (94%)
  local copies, waits for them, and re-layouts  3.34 us (5%)
    pallas_call x1, Pallas kernels, on_device(): pl.pallas_call(functools.partial(kernel, leaves * n_lon, n_lon, n_band),...  62.3 us
    unnamed x2, local copies, waits for them, and re-layouts  3.34 us

profile of v6, /device:TPU:0, one launch (start us, length us, event | category | flops | bytes accessed | tf_op | source)
XLA Modules:
  0.0 66.3 jit_solution(17917948754178232957)
XLA Ops:
  0.6 62.3 %shard_map.122 = (f32[16,16,256]{2,1,0:T(8,128)}, f32[16,16,256]{2,1,0:T(8,128)}) custom-call(f32[3,16,256]{2,1,0:T(8,128)} %pos_ref.1, f32[16,16,256]{2,1,0:T(8,128)} %sky_ref.1, f32[16,256]{1,0:T(8,128)} %noise_ref.1, f32[16,64,256]{2,1,0:T(8,128)} %bitcast.4, f32[16,4,64,64]{3,2,1,0:T(8,128)} %couple_ref.1, f32[16,64,64]{2,1,0:T(8,128)} %transfer_ref.1, ...), custom_call_target="tpu_custom_call" | custom-call | flops 335544320 | bytes 8388608 | tf_op jit(solution)/shard_map/pallas_call | solution.py:408
  62.9 1.7 %copy.15 = f32[16,16,256]{2,1,0:T(8,128)} copy(f32[16,16,256]{2,1,0:T(8,128)} %get-tuple-element.4) | data formatting | bytes 524288
  64.6 1.7 %copy.16 = f32[16,16,256]{2,1,0:T(8,128)} copy(f32[16,16,256]{2,1,0:T(8,128)} %get-tuple-element.5) | data formatting | bytes 524288
